TPU v7x, 256 devices: a whole 4x4x8 slice. The times are simulated.
256 devices in a mesh: lat: 8 (over y_hi, x), lon: 32 (over z, y_lo, core).
Axes of the slice: x: 4, y: 4 (y_hi: 2, y_lo: 2; y = y_hi * 2 + y_lo), z: 8, core: 2. Of those that a mesh axis runs over, the one named last changes fastest.
Arguments:
- queries: bfloat16 [128, 256, 768], P('lat', 'lon'), may hold values from -8 to 8
- key_vectors: bfloat16 [128, 256, 768], P('lat', 'lon'), may hold values from -8 to 8
- value_vectors: bfloat16 [128, 256, 768], P('lat', 'lon'), may hold values from -12 to 12
- upstream: bfloat16 [128, 256, 768], P('lat', 'lon'), may hold values from -6 to 6
- w_out: bfloat16 [768, 768], replicated, may hold values from -0.21875 to 0.21875
- neighbours: int32 [16, 32, 4], replicated, may hold values from 0 to 511, as said below
- counts: int32 [16, 32], replicated, may hold values from 2 to 4, as said below
Outputs:
- mixed_out: bfloat16 [128, 256, 768], P('lat', 'lon')
- q_grad: bfloat16 [128, 256, 768], P('lat', 'lon')
- k_grad: bfloat16 [128, 256, 768], P('lat', 'lon')
- v_grad: bfloat16 [128, 256, 768], P('lat', 'lon')
- w_grad: float32 [768, 768], replicated
Inputs may be any that keep to these rules, and one draw needn't show every extreme that they name: `neighbours`: entry s of block (i, j) names a block i2 * 32 + j2 with i2 within one of i and j2 within one of j around the longitude circle; slot 0 names the block itself, the entries of slots below counts[i, j] are distinct, and the slots at or beyond counts[i, j] name the block itself. `counts`: every block outside the first and the last row of blocks has 4.
All inputs are finite; a program needn't handle non-finite values.
Results may differ from a plain program's by a relative error of at most 0.03.
Values may be sent and summed in bfloat16 or wider, within the bound.
A program may use at most 64 MiB of HBM per device.

v0:
```python
import math
import jax
import jax.numpy as jnp
from jax import lax
from jax.sharding import PartitionSpec as P

HEADS = 12
HEAD_DIM = 64
BLK = 8
SLOTS = 4


def padded_2(value, sides, width, wrap):
    for axis, dim in sides:
        peers, length = (lax.axis_size(axis), value.shape[dim])
        up = [(i, (i + 1) % peers) for i in range(peers if wrap else peers - 1)]
        down = [(j, i) for i, j in up]
        last = lax.slice_in_dim(value, length - width, length, axis=dim)
        leading = lax.slice_in_dim(value, 0, width, axis=dim)
        before = lax.ppermute(last, axis, up)
        after = lax.ppermute(leading, axis, down)
        value = jnp.concatenate([before, value, after], axis=dim)
    return value


def to_blocks(token_grid):
    lat_rows, lon_cols, feat_width = token_grid.shape
    block_tiles = token_grid.reshape(
        lat_rows // BLK, BLK, lon_cols // BLK, BLK, feat_width
    ).transpose(0, 2, 1, 3, 4)
    return block_tiles.reshape(lat_rows // BLK * (lon_cols // BLK), BLK * BLK, feat_width)


def from_blocks(block_tiles, lat_blocks, lon_blocks):
    feat_width = block_tiles.shape[-1]
    token_grid = block_tiles.reshape(lat_blocks, lon_blocks, BLK, BLK, feat_width).transpose(
        0, 2, 1, 3, 4
    )
    return token_grid.reshape(lat_blocks * BLK, lon_blocks * BLK, feat_width)


def split_heads(block_tiles):
    return block_tiles.reshape(block_tiles.shape[0], block_tiles.shape[1], HEADS, HEAD_DIM)


def slot_places(
    neighbours,
    counts,
    first_lat,
    first_lon,
    grid_rows,
    grid_cols,
    anchor_lat,
    anchor_lon,
    pad_rows,
    pad_cols,
):
    total_lat = neighbours.shape[0]
    total_lon = neighbours.shape[1]
    block_lat = first_lat + jnp.arange(grid_rows, dtype=jnp.int32)
    block_lon = (first_lon + jnp.arange(grid_cols, dtype=jnp.int32)) % total_lon
    inside = (block_lat >= 0) & (block_lat < total_lat)
    safe_lat = jnp.clip(block_lat, 0, total_lat - 1)
    slot_table = jnp.take(jnp.take(neighbours, safe_lat, axis=0), block_lon, axis=1)
    slot_limit = jnp.take(jnp.take(counts, safe_lat, axis=0), block_lon, axis=1)
    slot_ids = jnp.arange(SLOTS, dtype=jnp.int32)
    rel_lat = slot_table // total_lon - anchor_lat
    rel_lon = (slot_table % total_lon - anchor_lon) % total_lon
    usable = (slot_ids[None, None, :] < slot_limit[:, :, None]) & inside[:, None, None]
    usable = usable & (rel_lat >= 0) & (rel_lat < pad_rows) & (rel_lon < pad_cols)
    key_place = jnp.where(usable, rel_lat * pad_cols + rel_lon, 0)
    return (
        key_place.reshape(grid_rows * grid_cols, SLOTS),
        usable.reshape(grid_rows * grid_cols, SLOTS),
    )


def gather_sets(padded_tiles, key_place):
    picked = jnp.take(padded_tiles, key_place.reshape(-1), axis=0)
    return picked.reshape(key_place.shape[0], SLOTS * BLK * BLK, padded_tiles.shape[-1])


def masked_scores(query_tiles, key_sets, key_valid):
    raw = jnp.einsum(
        "nqhd,nkhd->nhqk",
        split_heads(query_tiles),
        split_heads(key_sets),
        preferred_element_type=jnp.float32,
    )
    raw = raw * (1.0 / math.sqrt(HEAD_DIM))
    return jnp.where(key_valid[:, None, None, :], raw, -jnp.inf)


def forward_core(query_tiles, key_sets, value_sets, key_valid):
    masked = masked_scores(query_tiles, key_sets, key_valid)
    row_top = jnp.max(masked, axis=-1, keepdims=True)
    exp_total = jnp.sum(jnp.exp(masked - row_top), axis=-1, keepdims=True)
    log_total = row_top + jnp.log(exp_total)
    attn_probs = jnp.exp(masked - log_total)
    probs_low = attn_probs.astype(jnp.bfloat16)
    mixed_heads = jnp.einsum(
        "nhqk,nkhd->nqhd", probs_low, split_heads(value_sets), preferred_element_type=jnp.float32
    )
    attended = mixed_heads.astype(jnp.bfloat16).reshape(query_tiles.shape)
    return (attended, attn_probs, probs_low, log_total[..., 0])


def head_delta(d_att, attended):
    product = d_att.astype(jnp.float32) * attended.astype(jnp.float32)
    return jnp.sum(split_heads(product), axis=-1).transpose(0, 2, 1)


def backward_scores(attn_probs, d_att, row_delta, value_sets):
    dprobs = jnp.einsum(
        "nqhd,nkhd->nhqk",
        split_heads(d_att),
        split_heads(value_sets),
        preferred_element_type=jnp.float32,
    )
    return (attn_probs * (dprobs - row_delta[..., None]) * (1.0 / math.sqrt(HEAD_DIM))).astype(
        jnp.bfloat16
    )


def grad_queries(dscores, key_sets):
    summed = jnp.einsum(
        "nhqk,nkhd->nqhd", dscores, split_heads(key_sets), preferred_element_type=jnp.float32
    )
    return summed.astype(jnp.bfloat16).reshape(summed.shape[0], summed.shape[1], -1)


def contract_keys(weights_low, block_tiles):
    summed = jnp.einsum(
        "nhqk,nqhd->nkhd", weights_low, split_heads(block_tiles), preferred_element_type=jnp.float32
    )
    return summed.reshape(summed.shape[0], summed.shape[1], -1)


def add_into(contrib, key_place, usable, pad_count):
    flat_place = key_place.reshape(-1)
    feat_width = contrib.shape[-1]
    flat_terms = contrib.reshape(flat_place.shape[0], BLK * BLK * feat_width)
    flat_terms = jnp.where(usable.reshape(-1)[:, None], flat_terms, 0.0)
    summed = (
        jnp.zeros((pad_count, BLK * BLK * feat_width), jnp.float32).at[flat_place].add(flat_terms)
    )
    return summed.reshape(pad_count, BLK * BLK, feat_width)


def fold_lat(extended, lat_rows):
    interior = extended[:, 2 * BLK : 2 * BLK + lat_rows]
    interior = interior.at[:, :BLK].add(extended[:, :BLK])
    return interior.at[:, lat_rows - BLK :].add(extended[:, lat_rows + 3 * BLK :])


def fold_lon(extended, lon_cols):
    interior = extended[:, :, 2 * BLK : 2 * BLK + lon_cols]
    interior = interior.at[:, :, :BLK].add(extended[:, :, :BLK])
    return interior.at[:, :, lon_cols - BLK :].add(extended[:, :, lon_cols + 3 * BLK :])


def on_device(queries, key_vectors, value_vectors, upstream, w_out, neighbours, counts):
    lat_rows, lon_cols, feat_width = queries.shape
    lat_blocks = lat_rows // BLK
    lon_blocks = lon_cols // BLK
    pad_rows = lat_blocks + 2
    pad_cols = lon_blocks + 2
    pad_count = pad_rows * pad_cols
    inner_count = BLK * BLK
    tokens_all = lat_rows * lon_cols * lax.axis_size("lat") * lax.axis_size("lon")
    first_lat = lax.axis_index("lat") * lat_blocks
    first_lon = lax.axis_index("lon") * lon_blocks
    stacked = jnp.stack((key_vectors, value_vectors))
    lon_wide = padded_2(stacked, (("lon", 2),), BLK, True)
    padded = padded_2(lon_wide, (("lat", 1),), BLK, False)
    key_tiles = to_blocks(padded[0])
    value_tiles = to_blocks(padded[1])
    own_place, own_usable = slot_places(
        neighbours,
        counts,
        first_lat,
        first_lon,
        lat_blocks,
        lon_blocks,
        first_lat - 1,
        first_lon - 1,
        pad_rows,
        pad_cols,
    )
    query_tiles = to_blocks(queries)
    key_sets = gather_sets(key_tiles, own_place)
    value_sets = gather_sets(value_tiles, own_place)
    key_valid = jnp.repeat(own_usable, inner_count, axis=1)
    attended, attn_probs, probs_low, log_total = forward_core(
        query_tiles, key_sets, value_sets, key_valid
    )
    flat_att = attended.reshape(-1, feat_width)
    mixed_flat = jnp.dot(flat_att, w_out, preferred_element_type=jnp.float32).astype(jnp.bfloat16)
    grad_tiles = to_blocks(upstream)
    flat_grad = grad_tiles.reshape(-1, feat_width)
    local_weight = lax.dot_general(
        flat_att, flat_grad, (((0,), (0,)), ((), ())), preferred_element_type=jnp.float32
    )
    w_grad = lax.psum(local_weight, ("lat", "lon")) / math.sqrt(tokens_all)
    d_att = lax.dot_general(
        flat_grad, w_out, (((1,), (1,)), ((), ())), preferred_element_type=jnp.float32
    )
    d_att = d_att.astype(jnp.bfloat16).reshape(attended.shape)
    row_delta = head_delta(d_att, attended)
    dscores = backward_scores(attn_probs, d_att, row_delta, value_sets)
    query_grad = grad_queries(dscores, key_sets)
    key_contrib = contract_keys(dscores, query_tiles)
    value_contrib = contract_keys(probs_low, d_att)
    key_pad = from_blocks(
        add_into(key_contrib, own_place, own_usable, pad_count), pad_rows, pad_cols
    )
    value_pad = from_blocks(
        add_into(value_contrib, own_place, own_usable, pad_count), pad_rows, pad_cols
    )
    pad_terms = jnp.stack((key_pad, value_pad))
    extended = padded_2(pad_terms.astype(jnp.bfloat16), (("lat", 1),), BLK, False).astype(
        pad_terms.dtype
    )
    rows_done = fold_lat(extended, lat_rows)
    extended_lon = padded_2(rows_done.astype(jnp.bfloat16), (("lon", 2),), BLK, True).astype(
        rows_done.dtype
    )
    folded = fold_lon(extended_lon, lon_cols)
    key_grad = folded[0].astype(jnp.bfloat16)
    value_grad = folded[1].astype(jnp.bfloat16)
    mixed_out = from_blocks(mixed_flat.reshape(attended.shape), lat_blocks, lon_blocks)
    q_grad = from_blocks(query_grad, lat_blocks, lon_blocks)
    return (mixed_out, q_grad, key_grad, value_grad, w_grad)


def solution(mesh):
    return jax.shard_map(
        on_device,
        mesh=mesh,
        in_specs=(
            P("lat", "lon", None),
            P("lat", "lon", None),
            P("lat", "lon", None),
            P("lat", "lon", None),
            P(),
            P(),
            P(),
        ),
        out_specs=(
            P("lat", "lon", None),
            P("lat", "lon", None),
            P("lat", "lon", None),
            P("lat", "lon", None),
            P(),
        ),
        check_vma=False,
    )
```

profile of v0, /device:TPU:2, one launch (start us, length us, event | category | flops | bytes accessed | tf_op | source)
XLA Modules:
  0.0 395.0 jit_solution(1990365408183735528)
XLA Ops:
  7.2 1.2 pad_maximum_fusion.6
  8.4 6.4 %collective-permute-start.1 = (bf16[2,16,8,768]{3,2,1,0:T(8,128)(2,1)S(1)}, bf16[2,16,8,768]{3,2,1,0:T(8,128)(2,1)S(1)}, u32[]{:S(2)}, u32[]{:S(2)}) collective-permute-start(bf16[2,16,8,768]{3,2,1,0:T(8,128)(2,1)S(1)} %pad_maximum_fusion.6), channel_id=1, source_target_pairs={{1,0},{2,1},{3,2},{4,3},{5,4},{6,5},{7,6},{8,7},{9,8},{10,9},{11,1... | collective-permute-start | bytes 1179656 | tf_op jit(solution)/shard_map/ppermute | solution.py:21
  14.9 1.3 gather_fusion.1
  16.5 1.3 gather_fusion
  18.1 1.5 convolution_convert_fusion.2
  20.1 4.0 %collective-permute-done = bf16[2,16,8,768]{3,2,1,0:T(8,128)(2,1)S(1)} collective-permute-done((bf16[2,16,8,768]{3,2,1,0:T(8,128)(2,1)S(1)}, bf16[2,16,8,768]{3,2,1,0:T(8,128)(2,1)S(1)}, u32[]{:S(2)}, u32[]{:S(2)}) %collective-permute-start) | collective-permute-done | bytes 393248 | tf_op jit(solution)/shard_map/ppermute | solution.py:20
  25.3 2.4 collective-permute-start.3
  27.7 3.6 collective-permute-start.2
  31.9 1.1 copy.42
  33.4 1.2 copy.45
  35.3 2.5 collective-permute-done.3
  37.8 2.6 collective-permute-done.2
  40.5 1.4 pad_maximum_fusion
  42.3 1.5 gather_fusion.3
  43.7 1.5 gather_fusion.2
  45.2 2.5 broadcast_select_fusion.2
  47.7 2.7 reshape.642
  50.5 2.1 copy.37
  52.6 2.7 reshape.643
  55.4 2.1 copy.35
  57.5 1.8 bitcast_reduce_fusion
  61.0 1.3 multiply_reduce_fusion
  63.8 1.5 convolution_bitcast_fusion
  65.3 4.7 %copy.46 = f32[2,256,12,64]{3,2,1,0:T(8,128)} copy(f32[2,256,12,64]{1,3,2,0:T(8,128)} %convolution_bitcast_fusion) | data formatting | bytes 3145728 | tf_op jit(solution)/shard_map/nhqk,nqhd->nkhd/transpose | solution.py:133
  70.1 4.4 %reshape_reshape.37 = f32[8,49152]{1,0:T(8,128)} reshape(f32[2,256,12,64]{3,2,1,0:T(8,128)} %copy.46) | data formatting | bytes 3145728 | tf_op jit(solution)/shard_map/reshape;reshape | solution.py:142
  74.5 3.7 copy.49
  78.2 4.5 %reshape_reshape.39 = f32[8,49152]{1,0:T(8,128)} reshape(f32[2,256,12,64]{3,2,1,0:T(8,128)} %copy.49) | data formatting | bytes 3145728 | tf_op jit(solution)/shard_map/reshape;reshape | solution.py:142
  82.7 3.4 broadcast_select_fusion.1
  86.1 5.1 %scatter_custom_fusion.1 = f32[12,49152]{1,0:T(8,128)} fusion(s32[8]{0:T(128)} %fusion.29, f32[8,49152]{1,0:T(8,128)} %get-tuple-element.106, f32[]{:T(128)} %constant.271.clone.1), kind=kCustom, calls=%fused_computation.14 | custom fusion | flops 393216 | bytes 2359808 | tf_op jit(solution)/shard_map/scatter-add | solution.py:145
  91.2 2.0 convert.17
  93.8 4.9 %scatter_custom_fusion = f32[12,49152]{1,0:T(8,128)} fusion(s32[8]{0:T(128)} %fusion.29, f32[8,49152]{1,0:T(8,128)} %get-tuple-element.105, f32[]{:T(128)} %constant.271.clone.1), kind=kCustom, calls=%fused_computation.16 | custom fusion | flops 393216 | bytes 2359808 | tf_op jit(solution)/shard_map/scatter-add | solution.py:145
  98.7 2.0 convert.16
  101.2 1.1 pad_maximum_fusion.3
  102.4 1.9 collective-permute-start.5
  104.3 3.9 collective-permute-start.4
  108.3 1.2 copy.38
  109.4 1.9 reshape_reshape.35
  111.3 2.9 fusion.17
  114.5 1.9 collective-permute-done.4
  116.4 1.7 maximum_convert_fusion
  118.3 1.2 fusion.11
  119.5 1.3 fusion.10
  121.9 2.1 collective-permute-start.7
  126.8 2.8 collective-permute-done.7
  129.6 5.1 %collective-permute-done.6 = bf16[2,16,8,768]{3,2,1,0:T(8,128)(2,1)} collective-permute-done((bf16[2,16,8,768]{3,2,1,0:T(8,128)(2,1)}, bf16[2,16,8,768]{3,2,1,0:T(8,128)(2,1)}, u32[]{:S(2)}, u32[]{:S(2)}) %collective-permute-start.6) | collective-permute-done | bytes 393248 | tf_op jit(solution)/shard_map/ppermute | solution.py:20
  134.7 1.3 fusion.14
  136.8 248.1 %all-reduce.2.cloned.1.call-done = f32[768,768]{1,0:T(8,128)} async-done(((f32[768,768]{1,0:T(8,128)}), f32[768,768]{1,0:T(8,128)}) %all-reduce.2.cloned.1.call-update) | async-done | bytes 2359312 | tf_op jit(solution)/shard_map/psum | solution.py:204
  384.9 3.3 broadcast_multiply_fusion
  (77 shorter events, 13.8 us)
Async XLA Ops:
  7.2 11.0 %copy-start = (bf16[768,768]{1,0:T(8,128)(2,1)S(1)}, bf16[768,768]{1,0:T(8,128)(2,1)}, u32[]{:S(2)}) copy-start(bf16[768,768]{1,0:T(8,128)(2,1)} %param.25) | copy-start | bytes 3538948
  7.2 16.9 %copy-start.9 = (bf16[16,8,768]{2,1,0:T(8,128)(2,1)S(1)}, bf16[16,8,768]{2,1,0:T(8,128)(2,1)}, u32[]{:S(2)}) copy-start(bf16[16,8,768]{2,1,0:T(8,128)(2,1)} %param.23) | copy-start | bytes 589828
  7.2 16.9 %copy-start.10 = (bf16[16,8,768]{2,1,0:T(8,128)(2,1)S(1)}, bf16[16,8,768]{2,1,0:T(8,128)(2,1)}, u32[]{:S(2)}) copy-start(bf16[16,8,768]{2,1,0:T(8,128)(2,1)} %param.22) | copy-start | bytes 589828
  7.2 377.7 %all-reduce.2.cloned.1.call-start = ((), (), s32[]{:S(2)}) async-start(), calls=%async_computation | async-start | bytes 4718592 | tf_op jit(solution)/shard_map/psum | solution.py:204
  8.4 11.7 %collective-permute-start.1 = (bf16[2,16,8,768]{3,2,1,0:T(8,128)(2,1)S(1)}, bf16[2,16,8,768]{3,2,1,0:T(8,128)(2,1)S(1)}, u32[]{:S(2)}, u32[]{:S(2)}) collective-permute-start(bf16[2,16,8,768]{3,2,1,0:T(8,128)(2,1)S(1)} %pad_maximum_fusion.6), channel_id=1, source_target_pairs={{1,0},{2,1},{3,2},{4,3},{5,4},{6,5},{7,6},{8,7},{9,8},{10,9},{11,1... | collective-permute-start | bytes 1179656 | tf_op jit(solution)/shard_map/ppermute | solution.py:21
  14.8 9.3 %collective-permute-start = (bf16[2,16,8,768]{3,2,1,0:T(8,128)(2,1)S(1)}, bf16[2,16,8,768]{3,2,1,0:T(8,128)(2,1)S(1)}, u32[]{:S(2)}, u32[]{:S(2)}) collective-permute-start(bf16[2,16,8,768]{3,2,1,0:T(8,128)(2,1)S(1)} %pad_maximum_fusion.6), channel_id=1, source_target_pairs={{0,1},{1,2},{2,3},{3,4},{4,5},{5,6},{6,7},{7,8},{8,9},{9,10},{10,1... | collective-permute-start | bytes 1179656 | tf_op jit(solution)/shard_map/ppermute | solution.py:20
  24.2 8.9 %copy-start.13 = (bf16[16,8,768]{2,1,0:T(8,128)(2,1)S(1)}, bf16[16,8,768]{2,1,0:T(8,128)(2,1)}, u32[]{:S(2)}) copy-start(bf16[16,8,768]{2,1,0:T(8,128)(2,1)} %param.21) | copy-start | bytes 589828
  25.3 12.5 %collective-permute-start.3 = (bf16[2,8,24,768]{3,2,1,0:T(8,128)(2,1)}, bf16[2,8,24,768]{3,2,1,0:T(8,128)(2,1)}, u32[]{:S(2)}, u32[]{:S(2)}) collective-permute-start(bf16[2,8,24,768]{3,2,1,0:T(8,128)(2,1)} %get-tuple-element.102), channel_id=1, source_target_pairs={{32,0},{64,32},{96,64},{128,96},{160,128},{192,160},{224,192},{33,... | collective-permute-start | bytes 1769480 | tf_op jit(solution)/shard_map/ppermute | solution.py:21
  27.7 12.7 %collective-permute-start.2 = (bf16[2,8,24,768]{3,2,1,0:T(8,128)(2,1)}, bf16[2,8,24,768]{3,2,1,0:T(8,128)(2,1)}, u32[]{:S(2)}, u32[]{:S(2)}) collective-permute-start(bf16[2,8,24,768]{3,2,1,0:T(8,128)(2,1)} %get-tuple-element.101), channel_id=1, source_target_pairs={{0,32},{32,64},{64,96},{96,128},{128,160},{160,192},{192,224},{1,3... | collective-permute-start | bytes 1769480 | tf_op jit(solution)/shard_map/ppermute | solution.py:20
  43.7 1.5 copy-start.8
  57.5 2.4 copy-start.5
  59.9 1.1 copy-start.3
  62.2 1.6 copy-start.7
  62.9 0.9 copy-start.1
  78.2 4.6 %copy-start.6 = (f32[8,49152]{1,0:T(8,128)S(1)}, f32[8,49152]{1,0:T(8,128)}, u32[]{:S(2)}) copy-start(f32[8,49152]{1,0:T(8,128)} %reshape_reshape.37) | copy-start | bytes 4718596
  101.2 7.0 %copy-start.12 = (bf16[2,64,12,64]{1,3,2,0:T(8,128)(2,1)S(1)}, bf16[2,64,12,64]{1,3,2,0:T(8,128)(2,1)}, u32[]{:S(2)}) copy-start(bf16[2,64,12,64]{1,3,2,0:T(8,128)(2,1)} %get-tuple-element.114) | copy-start | bytes 589828
  102.4 12.1 %collective-permute-start.5 = (bf16[2,8,24,768]{3,2,1,0:T(8,128)(2,1)}, bf16[2,8,24,768]{3,2,1,0:T(8,128)(2,1)}, u32[]{:S(2)}, u32[]{:S(2)}) collective-permute-start(bf16[2,8,24,768]{3,2,1,0:T(8,128)(2,1)} %get-tuple-element.96), channel_id=1, source_target_pairs={{32,0},{64,32},{96,64},{128,96},{160,128},{192,160},{224,192},{33,... | collective-permute-start | bytes 1769480 | tf_op jit(solution)/shard_map/ppermute | solution.py:21
  104.3 12.1 %collective-permute-start.4 = (bf16[2,8,24,768]{3,2,1,0:T(8,128)(2,1)}, bf16[2,8,24,768]{3,2,1,0:T(8,128)(2,1)}, u32[]{:S(2)}, u32[]{:S(2)}) collective-permute-start(bf16[2,8,24,768]{3,2,1,0:T(8,128)(2,1)} %get-tuple-element.95), channel_id=1, source_target_pairs={{0,32},{32,64},{64,96},{96,128},{128,160},{160,192},{192,224},{1,3... | collective-permute-start | bytes 1769480 | tf_op jit(solution)/shard_map/ppermute | solution.py:20
  121.0 3.0 copy-start.2
  121.0 3.0 copy-start.4
  121.9 7.7 %collective-permute-start.7 = (bf16[2,16,8,768]{3,2,1,0:T(8,128)(2,1)}, bf16[2,16,8,768]{3,2,1,0:T(8,128)(2,1)}, u32[]{:S(2)}, u32[]{:S(2)}) collective-permute-start(bf16[2,16,8,768]{3,2,1,0:T(8,128)(2,1)} %get-tuple-element.100), channel_id=1, source_target_pairs={{1,0},{2,1},{3,2},{4,3},{5,4},{6,5},{7,6},{8,7},{9,8},{10,9},{11,1... | collective-permute-start | bytes 1179656 | tf_op jit(solution)/shard_map/ppermute | solution.py:21
  124.0 1.8 copy-start.11
  124.0 10.7 %collective-permute-start.6 = (bf16[2,16,8,768]{3,2,1,0:T(8,128)(2,1)}, bf16[2,16,8,768]{3,2,1,0:T(8,128)(2,1)}, u32[]{:S(2)}, u32[]{:S(2)}) collective-permute-start(bf16[2,16,8,768]{3,2,1,0:T(8,128)(2,1)} %get-tuple-element.99), channel_id=1, source_target_pairs={{0,1},{1,2},{2,3},{3,4},{4,5},{5,6},{6,7},{7,8},{8,9},{9,10},{10,1... | collective-permute-start | bytes 1179656 | tf_op jit(solution)/shard_map/ppermute | solution.py:20
Sparse Core Ops, SparseCore 0:
  114.3 270.4 all-reduce.1
where the time goes:
time: 396 us; the launch traced here: 395 us
  waiting for transfers between devices  268 us (68%)
  local copies, waits for them, and re-layouts  46.5 us (12%)
  other arithmetic  34.4 us (9%)
  starting transfers between devices  20.4 us (5%)
  between operations  14.4 us (4%)
  matrix products  11.4 us (3%)
    psum x1, waiting for transfers between devices, on_device(): w_grad = lax.psum(local_weight, ('lat', 'lon')) / math.sqrt(tokens_all)  248 us
    ppermute x4, waiting for transfers between devices, padded_2(): before = lax.ppermute(last, axis, up)  13.7 us
    ppermute x4, starting transfers between devices, padded_2(): after = lax.ppermute(leading, axis, down)  12.8 us
    another operation x8, local copies, waits for them, and re-layouts, split_heads(): block_tiles.reshape(block_tiles.shape[0], block_tiles.shape[1], HEADS, HE...  12.7 us
    scatter-add x2, other arithmetic, add_into(): jnp.zeros((pad_count, BLK * BLK * feat_width), jnp.float32).at[flat_place]  10 us
    another operation x2, local copies, waits for them, and re-layouts, add_into(): flat_terms = contrib.reshape(flat_place.shape[0], BLK * BLK * feat_width)  8.94 us
    transpose x2, local copies, waits for them, and re-layouts, contract_keys(): jnp.einsum('nhqk,nqhd->nkhd', weights_low, split_heads(block_tiles), pref...  8.45 us
  transfers between devices with their start and end apart: 9, of which 9 were waited for; matrix products, arithmetic and copies ran while one was open for 6% of the time, Pallas kernels for 0%

commit v1 on v0

--- a/solution.py
+++ b/solution.py
@@ -8,6 +8,11 @@
 HEAD_DIM = 64
 BLK = 8
 SLOTS = 4
+
+
+def one_after_other(array, first, second):
+    inner = lax.psum(array, first)
+    return lax.psum(inner, second)
 
 
 def padded_2(value, sides, width, wrap):
@@ -201,7 +206,7 @@
     local_weight = lax.dot_general(
         flat_att, flat_grad, (((0,), (0,)), ((), ())), preferred_element_type=jnp.float32
     )
-    w_grad = lax.psum(local_weight, ("lat", "lon")) / math.sqrt(tokens_all)
+    w_grad = one_after_other(local_weight, "lat", "lon") / math.sqrt(tokens_all)
     d_att = lax.dot_general(
         flat_grad, w_out, (((1,), (1,)), ((), ())), preferred_element_type=jnp.float32
     )

time: 396 us -> 443 us (1.12)
  waiting for transfers between devices: 268 us -> 316 us
    psum x1 -> x2, waiting for transfers between devices: 248 us -> 300 us  [the longest x1 218 us: one_after_other(): return lax.psum(inner, second)]
  transfers between devices with their start and end apart: 9 -> 10, of which waited for: 9 -> 8; matrix products, arithmetic and copies ran while one was open for 6% -> 9% of each run, Pallas kernels for 0% -> 0%
where the time goes in v1:
time: 443 us; the launch traced here: 442 us
  waiting for transfers between devices  316 us (71%)
  local copies, waits for them, and re-layouts  46.6 us (11%)
  other arithmetic  35 us (8%)
  starting transfers between devices  18.6 us (4%)
  between operations  14.4 us (3%)
  matrix products  11.3 us (3%)
    psum x1, waiting for transfers between devices, one_after_other(): return lax.psum(inner, second)  218 us
    psum x1, waiting for transfers between devices, one_after_other(): inner = lax.psum(array, first)  81.8 us
    another operation x8, local copies, waits for them, and re-layouts, split_heads(): block_tiles.reshape(block_tiles.shape[0], block_tiles.shape[1], HEADS, HE...  12.7 us
    ppermute x4, starting transfers between devices, padded_2(): after = lax.ppermute(leading, axis, down)  10.7 us
    ppermute x4, waiting for transfers between devices, padded_2(): before = lax.ppermute(last, axis, up)  10.7 us
    scatter-add x2, other arithmetic, add_into(): jnp.zeros((pad_count, BLK * BLK * feat_width), jnp.float32).at[flat_place]  10.1 us
    another operation x2, local copies, waits for them, and re-layouts, add_into(): flat_terms = contrib.reshape(flat_place.shape[0], BLK * BLK * feat_width)  9.09 us
  transfers between devices with their start and end apart: 10, of which 8 were waited for; matrix products, arithmetic and copies ran while one was open for 9% of the time, Pallas kernels for 0%

profile of v1, /device:TPU:2, one launch (start us, length us, event | category | flops | bytes accessed | tf_op | source)
XLA Modules:
  0.0 441.6 jit_solution(17331855381126839834)
XLA Ops:
  7.2 1.2 pad_maximum_fusion.6
  8.4 6.4 %collective-permute-start.1 = (bf16[2,16,8,768]{3,2,1,0:T(8,128)(2,1)S(1)}, bf16[2,16,8,768]{3,2,1,0:T(8,128)(2,1)S(1)}, u32[]{:S(2)}, u32[]{:S(2)}) collective-permute-start(bf16[2,16,8,768]{3,2,1,0:T(8,128)(2,1)S(1)} %pad_maximum_fusion.6), channel_id=1, source_target_pairs={{1,0},{2,1},{3,2},{4,3},{5,4},{6,5},{7,6},{8,7},{9,8},{10,9},{11,1... | collective-permute-start | bytes 1179656 | tf_op jit(solution)/shard_map/ppermute | solution.py:26
  14.9 1.3 gather_fusion.1
  16.5 1.3 gather_fusion
  18.1 1.5 convolution_convert_fusion.2
  20.1 4.0 collective-permute-done
  25.3 2.4 collective-permute-start.3
  27.7 3.4 collective-permute-start.2
  31.8 1.1 copy.42
  33.2 1.2 copy.45
  35.6 2.2 collective-permute-done.3
  37.8 2.6 collective-permute-done.2
  40.5 1.4 pad_maximum_fusion
  42.3 1.5 gather_fusion.3
  43.7 1.5 gather_fusion.2
  45.2 2.5 broadcast_select_fusion.2
  47.7 2.7 reshape.642
  50.5 2.1 copy.37
  52.6 2.7 reshape.643
  55.4 2.2 copy.35
  57.5 1.8 bitcast_reduce_fusion
  59.9 1.6 convolution_bitcast_fusion.1
  62.6 1.2 copy.38
  63.8 1.9 reshape_reshape.35
  65.7 1.7 multiply_convert_fusion
  68.7 3.7 copy.46
  72.4 4.6 %reshape_reshape.37 = f32[8,49152]{1,0:T(8,128)} reshape(f32[2,256,12,64]{3,2,1,0:T(8,128)} %copy.46) | data formatting | bytes 3145728 | tf_op jit(solution)/shard_map/reshape;reshape | solution.py:147
  77.0 3.7 copy.49
  80.7 4.5 %reshape_reshape.39 = f32[8,49152]{1,0:T(8,128)} reshape(f32[2,256,12,64]{3,2,1,0:T(8,128)} %copy.49) | data formatting | bytes 3145728 | tf_op jit(solution)/shard_map/reshape;reshape | solution.py:147
  85.3 1.9 fusion.17
  87.2 1.3 copy-done.7
  88.6 3.4 broadcast_select_fusion.1
  91.9 5.1 %scatter_custom_fusion.1 = f32[12,49152]{1,0:T(8,128)} fusion(s32[8]{0:T(128)} %fusion.29, f32[8,49152]{1,0:T(8,128)} %get-tuple-element.106, f32[]{:T(128)} %constant.271.clone.1), kind=kCustom, calls=%fused_computation.14 | custom fusion | flops 393216 | bytes 2359808 | tf_op jit(solution)/shard_map/scatter-add | solution.py:150
  97.1 2.0 convert.17
  99.6 4.9 %scatter_custom_fusion = f32[12,49152]{1,0:T(8,128)} fusion(s32[8]{0:T(128)} %fusion.29, f32[8,49152]{1,0:T(8,128)} %get-tuple-element.105, f32[]{:T(128)} %constant.271.clone.1), kind=kCustom, calls=%fused_computation.16 | custom fusion | flops 393216 | bytes 2359808 | tf_op jit(solution)/shard_map/scatter-add | solution.py:150
  104.6 2.1 convert.16
  107.1 1.2 pad_maximum_fusion.3
  108.3 1.9 collective-permute-start.5
  110.2 3.9 collective-permute-start.4
  114.2 81.8 %all-reduce.3.cloned.1.call-done = f32[768,768]{1,0:T(8,128)} async-done(((f32[768,768]{1,0:T(8,128)}), f32[768,768]{1,0:T(8,128)}) %all-reduce.3.cloned.1.call-update) | async-done | bytes 2359312 | tf_op jit(solution)/shard_map/psum | solution.py:14
  196.0 1.7 maximum_convert_fusion
  197.9 1.2 fusion.11
  199.1 1.3 fusion.10
  205.0 2.1 collective-permute-done.7
  207.1 4.1 collective-permute-done.6
  211.2 1.3 fusion.14
  213.3 218.2 %all-reduce.5.cloned.1.call-done = f32[768,768]{1,0:T(8,128)} async-done(((f32[768,768]{1,0:T(8,128)}), f32[768,768]{1,0:T(8,128)}) %all-reduce.5.cloned.1.call-update) | async-done | bytes 2359312 | tf_op jit(solution)/shard_map/psum | solution.py:15
  431.4 3.3 broadcast_multiply_fusion
  (86 shorter events, 14.4 us)
Async XLA Ops:
  7.2 11.0 %copy-start = (bf16[768,768]{1,0:T(8,128)(2,1)S(1)}, bf16[768,768]{1,0:T(8,128)(2,1)}, u32[]{:S(2)}) copy-start(bf16[768,768]{1,0:T(8,128)(2,1)} %param.25) | copy-start | bytes 3538948
  7.2 16.9 %copy-start.10 = (bf16[16,8,768]{2,1,0:T(8,128)(2,1)S(1)}, bf16[16,8,768]{2,1,0:T(8,128)(2,1)}, u32[]{:S(2)}) copy-start(bf16[16,8,768]{2,1,0:T(8,128)(2,1)} %param.23) | copy-start | bytes 589828
  7.2 16.9 %copy-start.11 = (bf16[16,8,768]{2,1,0:T(8,128)(2,1)S(1)}, bf16[16,8,768]{2,1,0:T(8,128)(2,1)}, u32[]{:S(2)}) copy-start(bf16[16,8,768]{2,1,0:T(8,128)(2,1)} %param.22) | copy-start | bytes 589828
  7.2 188.7 %all-reduce.3.cloned.1.call-start = ((), (), s32[]{:S(2)}) async-start(), calls=%async_computation | async-start | bytes 4718592 | tf_op jit(solution)/shard_map/psum | solution.py:14
  8.4 11.7 %collective-permute-start.1 = (bf16[2,16,8,768]{3,2,1,0:T(8,128)(2,1)S(1)}, bf16[2,16,8,768]{3,2,1,0:T(8,128)(2,1)S(1)}, u32[]{:S(2)}, u32[]{:S(2)}) collective-permute-start(bf16[2,16,8,768]{3,2,1,0:T(8,128)(2,1)S(1)} %pad_maximum_fusion.6), channel_id=1, source_target_pairs={{1,0},{2,1},{3,2},{4,3},{5,4},{6,5},{7,6},{8,7},{9,8},{10,9},{11,1... | collective-permute-start | bytes 1179656 | tf_op jit(solution)/shard_map/ppermute | solution.py:26
  14.8 9.3 %collective-permute-start = (bf16[2,16,8,768]{3,2,1,0:T(8,128)(2,1)S(1)}, bf16[2,16,8,768]{3,2,1,0:T(8,128)(2,1)S(1)}, u32[]{:S(2)}, u32[]{:S(2)}) collective-permute-start(bf16[2,16,8,768]{3,2,1,0:T(8,128)(2,1)S(1)} %pad_maximum_fusion.6), channel_id=1, source_target_pairs={{0,1},{1,2},{2,3},{3,4},{4,5},{5,6},{6,7},{7,8},{8,9},{9,10},{10,1... | collective-permute-start | bytes 1179656 | tf_op jit(solution)/shard_map/ppermute | solution.py:25
  24.2 8.7 %copy-start.15 = (bf16[16,8,768]{2,1,0:T(8,128)(2,1)S(1)}, bf16[16,8,768]{2,1,0:T(8,128)(2,1)}, u32[]{:S(2)}) copy-start(bf16[16,8,768]{2,1,0:T(8,128)(2,1)} %param.21) | copy-start | bytes 589828
  25.3 12.5 %collective-permute-start.3 = (bf16[2,8,24,768]{3,2,1,0:T(8,128)(2,1)}, bf16[2,8,24,768]{3,2,1,0:T(8,128)(2,1)}, u32[]{:S(2)}, u32[]{:S(2)}) collective-permute-start(bf16[2,8,24,768]{3,2,1,0:T(8,128)(2,1)} %get-tuple-element.102), channel_id=1, source_target_pairs={{32,0},{64,32},{96,64},{128,96},{160,128},{192,160},{224,192},{33,... | collective-permute-start | bytes 1769480 | tf_op jit(solution)/shard_map/ppermute | solution.py:26
  27.7 12.7 %collective-permute-start.2 = (bf16[2,8,24,768]{3,2,1,0:T(8,128)(2,1)}, bf16[2,8,24,768]{3,2,1,0:T(8,128)(2,1)}, u32[]{:S(2)}, u32[]{:S(2)}) collective-permute-start(bf16[2,8,24,768]{3,2,1,0:T(8,128)(2,1)} %get-tuple-element.101), channel_id=1, source_target_pairs={{0,32},{32,64},{64,96},{96,128},{128,160},{160,192},{192,224},{1,3... | collective-permute-start | bytes 1769480 | tf_op jit(solution)/shard_map/ppermute | solution.py:25
  43.7 1.5 copy-start.9
  57.5 2.4 copy-start.5
  59.9 1.6 copy-start.3
  65.7 2.6 copy-start.8
  67.4 0.9 copy-start.1
  72.4 4.6 %copy-start.6 = (f32[2,256,12,64]{1,3,2,0:T(8,128)S(1)}, f32[2,256,12,64]{1,3,2,0:T(8,128)}, u32[]{:S(2)}) copy-start(f32[2,256,12,64]{1,3,2,0:T(8,128)} %convolution_bitcast_fusion.1) | copy-start | bytes 4718596
  80.7 4.5 %copy-start.12 = (bf16[128,768]{0,1:T(8,128)(2,1)S(1)}, bf16[128,768]{0,1:T(8,128)(2,1)}, u32[]{:S(2)}) copy-start(bf16[128,768]{0,1:T(8,128)(2,1)} %reshape_reshape.35) | copy-start | bytes 589828
  80.7 4.5 %copy-start.14 = (bf16[16,8,768]{2,1,0:T(8,128)(2,1)S(1)}, bf16[16,8,768]{2,1,0:T(8,128)(2,1)}, u32[]{:S(2)}) copy-start(bf16[16,8,768]{2,1,0:T(8,128)(2,1)} %param.24) | copy-start | bytes 589828
  87.1 1.4 copy-start.7
  87.1 1.4 copy-start.16
  87.2 344.3 %all-reduce.5.cloned.1.call-start = ((), (), s32[]{:S(2)}) async-start(), calls=%async_computation.1 | async-start | bytes 4718592 | tf_op jit(solution)/shard_map/psum | solution.py:15
  108.3 87.6 %collective-permute-start.5 = (bf16[2,8,24,768]{3,2,1,0:T(8,128)(2,1)}, bf16[2,8,24,768]{3,2,1,0:T(8,128)(2,1)}, u32[]{:S(2)}, u32[]{:S(2)}) collective-permute-start(bf16[2,8,24,768]{3,2,1,0:T(8,128)(2,1)} %get-tuple-element.96), channel_id=1, source_target_pairs={{32,0},{64,32},{96,64},{128,96},{160,128},{192,160},{224,192},{33,... | collective-permute-start | bytes 1769480 | tf_op jit(solution)/shard_map/ppermute | solution.py:26
  110.2 85.7 %collective-permute-start.4 = (bf16[2,8,24,768]{3,2,1,0:T(8,128)(2,1)}, bf16[2,8,24,768]{3,2,1,0:T(8,128)(2,1)}, u32[]{:S(2)}, u32[]{:S(2)}) collective-permute-start(bf16[2,8,24,768]{3,2,1,0:T(8,128)(2,1)} %get-tuple-element.95), channel_id=1, source_target_pairs={{0,32},{32,64},{64,96},{96,128},{128,160},{160,192},{192,224},{1,3... | collective-permute-start | bytes 1769480 | tf_op jit(solution)/shard_map/ppermute | solution.py:25
  200.5 1.5 copy-start.2
  200.5 1.6 copy-start.4
  201.5 5.7 %collective-permute-start.7 = (bf16[2,16,8,768]{3,2,1,0:T(8,128)(2,1)}, bf16[2,16,8,768]{3,2,1,0:T(8,128)(2,1)}, u32[]{:S(2)}, u32[]{:S(2)}) collective-permute-start(bf16[2,16,8,768]{3,2,1,0:T(8,128)(2,1)} %get-tuple-element.100), channel_id=1, source_target_pairs={{1,0},{2,1},{3,2},{4,3},{5,4},{6,5},{7,6},{8,7},{9,8},{10,9},{11,1... | collective-permute-start | bytes 1179656 | tf_op jit(solution)/shard_map/ppermute | solution.py:26
  201.5 2.5 copy-start.13
  201.5 9.7 %collective-permute-start.6 = (bf16[2,16,8,768]{3,2,1,0:T(8,128)(2,1)}, bf16[2,16,8,768]{3,2,1,0:T(8,128)(2,1)}, u32[]{:S(2)}, u32[]{:S(2)}) collective-permute-start(bf16[2,16,8,768]{3,2,1,0:T(8,128)(2,1)} %get-tuple-element.99), channel_id=1, source_target_pairs={{0,1},{1,2},{2,3},{3,4},{4,5},{5,6},{6,7},{7,8},{8,9},{9,10},{10,1... | collective-permute-start | bytes 1179656 | tf_op jit(solution)/shard_map/ppermute | solution.py:25
Sparse Core Ops, SparseCore 0:
  87.3 108.5 all-reduce.2
  198.6 232.8 all-reduce.4
